TPU v7x, 256 devices: a whole 4x4x8 slice. The times are simulated.
256 devices in a mesh: section: 2 (over x_lo), row: 16 (over y, x_hi, core), col: 8 (over z).
Axes of the slice: x: 4 (x_hi: 2, x_lo: 2; x = x_hi * 2 + x_lo), y: 4, z: 8, core: 2. Of those that a mesh axis runs over, the one named last changes fastest.
Arguments:
- fwd_in: bfloat16 [2, 384, 8192], P('section', 'col', 'row'), may hold values from -6 to 6
- bwd_in: bfloat16 [2, 384, 8192], P('section', 'col', 'row'), may hold values from -6 to 6
- cotangent: bfloat16 [2, 384, 8192], P('section', 'col', 'row'), may hold values from -6 to 6
- w_gate: bfloat16 [2, 8192, 14336], P('section', 'row', 'col'), may hold values from -0.0625 to 0.0625
- w_up: bfloat16 [2, 8192, 14336], P('section', 'row', 'col'), may hold values from -0.0625 to 0.0625
- w_down: bfloat16 [2, 14336, 8192], P('section', 'col', 'row'), may hold values from -0.046875 to 0.046875
Outputs:
- next_inputs: bfloat16 [2, 384, 8192], P('section', ('row', 'col'))
- next_grads: bfloat16 [2, 384, 8192], P('section', ('row', 'col'))
- grad_gate: bfloat16 [2, 8192, 14336], P('section', 'row', 'col')
- grad_up: bfloat16 [2, 8192, 14336], P('section', 'row', 'col')
- grad_down: bfloat16 [2, 14336, 8192], P('section', 'col', 'row')
All inputs are finite; a program needn't handle non-finite values.
Results may differ from a plain program's by a relative error of at most 0.027.
Values may be sent and summed in bfloat16 or wider, within the bound.
A program may use at most 64 MiB of HBM per device.

v0:
```python
import jax
import jax.numpy as jnp
from jax import lax
from jax.sharding import PartitionSpec as P


def from_behind(block, axis, distance):
    devices = range(lax.axis_size(axis))
    route = [((i - distance) % len(devices), i) for i in devices]
    return lax.ppermute(block, axis, route)


def product(left, right):
    return jnp.dot(left, right, preferred_element_type=jnp.float32)


def against(left, right, dims):
    return lax.dot_general(
        left, right, (((dims[0],), (dims[1],)), ((), ())), preferred_element_type=jnp.float32
    )


def activate(gate_new, up_new, gate_old, up_old, d_act):
    sig_new = jax.nn.sigmoid(gate_new)
    sig_old = jax.nn.sigmoid(gate_old)
    act_new = (gate_new * sig_new * up_new).astype(jnp.bfloat16)
    act_old = (gate_old * sig_old * up_old).astype(jnp.bfloat16)
    d_gate = (d_act * up_old * sig_old * (1.0 + gate_old * (1.0 - sig_old))).astype(jnp.bfloat16)
    d_up = (d_act * gate_old * sig_old).astype(jnp.bfloat16)
    return (act_new, act_old, d_gate, d_up)


def with_residual(partial_term, local, col_index):
    count = local.shape[0]
    piece = lax.dynamic_slice_in_dim(partial_term, col_index * count, count, 0) + local.astype(
        jnp.float32
    )
    return lax.dynamic_update_slice_in_dim(partial_term, piece, col_index * count, 0)


def regroup(partial_term, rows_axis, cols_axis):
    tokens, width = partial_term.shape
    small = tokens // (rows_axis * cols_axis)
    shaped = partial_term.reshape(rows_axis, cols_axis, small, width)
    return jnp.transpose(shaped, (1, 0, 2, 3)).reshape(cols_axis * rows_axis, small, width)


def body(fwd_in, bwd_in, cotangent, w_gate, w_up, w_down):
    fresh = fwd_in[0]
    stored = bwd_in[0]
    incoming = cotangent[0]
    gate_weight = w_gate[0]
    up_weight = w_up[0]
    down_weight = w_down[0]
    rows_axis = lax.axis_size("row")
    cols_axis = lax.axis_size("col")
    col_index = lax.axis_index("col")
    fresh_all, stored_all, incoming_all = (
        lax.all_gather(fresh, "col", axis=0, tiled=True),
        lax.all_gather(stored, "col", axis=0, tiled=True),
        lax.all_gather(incoming, "col", axis=0, tiled=True),
    )
    gate_new = product(fresh_all, gate_weight)
    up_new = product(fresh_all, up_weight)
    gate_old = product(stored_all, gate_weight)
    up_old = product(stored_all, up_weight)
    d_act = against(incoming_all, down_weight, (1, 1))
    sums = (
        lax.psum_scatter(
            gate_new.astype(jnp.bfloat16), "row", scatter_dimension=0, tiled=True
        ).astype(jnp.float32),
        lax.psum_scatter(
            up_new.astype(jnp.bfloat16), "row", scatter_dimension=0, tiled=True
        ).astype(jnp.float32),
        lax.psum_scatter(
            gate_old.astype(jnp.bfloat16), "row", scatter_dimension=0, tiled=True
        ).astype(jnp.float32),
        lax.psum_scatter(
            up_old.astype(jnp.bfloat16), "row", scatter_dimension=0, tiled=True
        ).astype(jnp.float32),
        lax.psum_scatter(d_act.astype(jnp.bfloat16), "row", scatter_dimension=0, tiled=True).astype(
            jnp.float32
        ),
    )
    local_parts = activate(sums[0], sums[1], sums[2], sums[3], sums[4])
    act_new, act_old, d_gate, d_up = (
        lax.all_gather(local_parts[0], "row", axis=0, tiled=True),
        lax.all_gather(local_parts[1], "row", axis=0, tiled=True),
        lax.all_gather(local_parts[2], "row", axis=0, tiled=True),
        lax.all_gather(local_parts[3], "row", axis=0, tiled=True),
    )
    out_part = with_residual(product(act_new, down_weight), fresh, col_index)
    grad_part = with_residual(
        against(d_gate, gate_weight, (1, 1)) + against(d_up, up_weight, (1, 1)), incoming, col_index
    )
    out_sum, grad_sum = (
        lax.psum_scatter(
            regroup(out_part, rows_axis, cols_axis).astype(jnp.bfloat16),
            "col",
            scatter_dimension=0,
            tiled=True,
        ).astype(jnp.float32),
        lax.psum_scatter(
            regroup(grad_part, rows_axis, cols_axis).astype(jnp.bfloat16),
            "col",
            scatter_dimension=0,
            tiled=True,
        ).astype(jnp.float32),
    )
    layer_out = out_sum.astype(jnp.bfloat16)
    input_grad = grad_sum.astype(jnp.bfloat16)
    wide_out, wide_grad = (
        lax.all_gather(layer_out, "row", axis=2, tiled=True),
        lax.all_gather(input_grad, "row", axis=2, tiled=True),
    )
    row_index = lax.axis_index("row")
    whole_out = lax.dynamic_index_in_dim(wide_out, row_index, 0, keepdims=False)
    whole_grad = lax.dynamic_index_in_dim(wide_grad, row_index, 0, keepdims=False)
    grad_gate = against(stored_all, d_gate, (0, 0)).astype(jnp.bfloat16)
    grad_up = against(stored_all, d_up, (0, 0)).astype(jnp.bfloat16)
    grad_down = against(act_old, incoming_all, (0, 0)).astype(jnp.bfloat16)
    moved_out, moved_grad = from_behind((whole_out, whole_grad), "section", 1)
    return (moved_out[None], moved_grad[None], grad_gate[None], grad_up[None], grad_down[None])


def solution(mesh):
    in_specs = (
        P("section", "col", "row"),
        P("section", "col", "row"),
        P("section", "col", "row"),
        P("section", "row", "col"),
        P("section", "row", "col"),
        P("section", "col", "row"),
    )
    out_specs = (
        P("section", ("row", "col"), None),
        P("section", ("row", "col"), None),
        P("section", "row", "col"),
        P("section", "row", "col"),
        P("section", "col", "row"),
    )
    return jax.shard_map(body, mesh=mesh, in_specs=in_specs, out_specs=out_specs, check_vma=False)
```

profile of v0, /device:TPU:1, one launch (start us, length us, event | category | flops | bytes accessed | tf_op | source)
XLA Modules:
  0.0 736.0 jit_solution(4353792958260038700)
XLA Ops:
  7.2 23.9 %all-gather.2 = bf16[1,384,512]{2,1,0:T(8,128)(2,1)S(1)} all-gather(bf16[1,48,512]{2,1,0:T(8,128)(2,1)} %param.7), channel_id=4, replica_groups=mesh['section'=2,'row'=16,'col'=8] {'col'}, dimensions={1}, use_global_device_ids=true | all-gather | bytes 442368 | tf_op jit(solution)/shard_map/all_gather | solution.py:60
  31.1 2.0 convolution_convert_fusion.4
  33.2 3.5 convolution_convert_fusion.3
  36.7 18.7 %all-gather.1 = bf16[1,384,512]{2,1,0:T(8,128)(2,1)S(1)} all-gather(bf16[1,48,512]{2,1,0:T(8,128)(2,1)S(1)} %copy-done.1), channel_id=3, replica_groups=mesh['section'=2,'row'=16,'col'=8] {'col'}, dimensions={1}, use_global_device_ids=true | all-gather | bytes 442368 | tf_op jit(solution)/shard_map/all_gather | solution.py:61
  55.4 3.6 convolution_convert_fusion.5
  59.0 18.8 %all-gather = bf16[1,384,512]{2,1,0:T(8,128)(2,1)S(1)} all-gather(bf16[1,48,512]{2,1,0:T(8,128)(2,1)S(1)} %copy-done.2), channel_id=2, replica_groups=mesh['section'=2,'row'=16,'col'=8] {'col'}, dimensions={1}, use_global_device_ids=true | all-gather | bytes 442368 | tf_op jit(solution)/shard_map/all_gather | solution.py:59
  77.8 2.0 convolution_convert_fusion.6
  79.8 3.5 convolution_convert_fusion.7
  83.3 28.5 %reduce-scatter.16.cloned.1.call-done = bf16[24,1792]{1,0:T(8,128)(2,1)} async-done(((bf16[384,1792]{1,0:T(8,128)(2,1)}), bf16[24,1792]{1,0:T(8,128)(2,1)}) %reduce-scatter.16.cloned.1.call-update) | async-done | bytes 86032 | tf_op jit(solution)/shard_map/reduce_scatter | solution.py:78
  111.9 78.5 %reduce-scatter.18.cloned.1.call-done = bf16[24,1792]{1,0:T(8,128)(2,1)} async-done(((bf16[384,1792]{1,0:T(8,128)(2,1)}), bf16[24,1792]{1,0:T(8,128)(2,1)}) %reduce-scatter.18.cloned.1.call-update) | async-done | bytes 86032 | tf_op jit(solution)/shard_map/reduce_scatter | solution.py:75
  190.4 78.5 %reduce-scatter.14.cloned.1.call-done = bf16[24,1792]{1,0:T(8,128)(2,1)} async-done(((bf16[384,1792]{1,0:T(8,128)(2,1)}), bf16[24,1792]{1,0:T(8,128)(2,1)}) %reduce-scatter.14.cloned.1.call-update) | async-done | bytes 86032 | tf_op jit(solution)/shard_map/reduce_scatter | solution.py:81
  268.8 1.8 fusion.32
  271.4 76.4 %reduce-scatter.10.cloned.1.call-done = bf16[24,1792]{1,0:T(8,128)(2,1)} async-done(((bf16[384,1792]{1,0:T(8,128)(2,1)}), bf16[24,1792]{1,0:T(8,128)(2,1)}) %reduce-scatter.10.cloned.1.call-update) | async-done | bytes 86032 | tf_op jit(solution)/shard_map/reduce_scatter | solution.py:72
  347.8 79.0 %reduce-scatter.8.cloned.1.call-done = bf16[24,1792]{1,0:T(8,128)(2,1)} async-done(((bf16[384,1792]{1,0:T(8,128)(2,1)}), bf16[24,1792]{1,0:T(8,128)(2,1)}) %reduce-scatter.8.cloned.1.call-update) | async-done | bytes 86032 | tf_op jit(solution)/shard_map/reduce_scatter | solution.py:69
  426.7 1.6 fusion.39
  428.4 52.9 %all-gather.12.cloned.1.call-done = bf16[384,1792]{1,0:T(8,128)(2,1)} async-done(((bf16[24,1792]{1,0:T(8,128)(2,1)}), bf16[384,1792]{1,0:T(8,128)(2,1)}) %all-gather.12.cloned.1.call-update) | async-done | bytes 1376272 | tf_op jit(solution)/shard_map/all_gather | solution.py:90
  481.4 2.2 fusion.6
  483.6 50.6 %all-gather.10.cloned.1.call-done = bf16[384,1792]{1,0:T(8,128)(2,1)} async-done(((bf16[24,1792]{1,0:T(8,128)(2,1)}), bf16[384,1792]{1,0:T(8,128)(2,1)}) %all-gather.10.cloned.1.call-update) | async-done | bytes 1376272 | tf_op jit(solution)/shard_map/all_gather | solution.py:89
  534.2 2.8 fusion.14
  537.4 1.0 copy.18
  538.5 48.6 %all-gather.8.cloned.1.call-done = bf16[384,1792]{1,0:T(8,128)(2,1)} async-done(((bf16[24,1792]{1,0:T(8,128)(2,1)}), bf16[384,1792]{1,0:T(8,128)(2,1)}) %all-gather.8.cloned.1.call-update) | async-done | bytes 1376272 | tf_op jit(solution)/shard_map/all_gather | solution.py:87
  587.1 2.8 fusion.4
  592.0 3.8 fusion
  595.9 2.4 fusion.1
  598.2 22.7 %reduce-scatter.20.cloned.1.call-done = bf16[16,3,512]{2,0,1:T(8,128)(2,1)} async-done(((bf16[128,3,512]{2,0,1:T(8,128)(2,1)}), bf16[16,3,512]{2,0,1:T(8,128)(2,1)}) %reduce-scatter.20.cloned.1.call-update) | async-done | bytes 49168 | tf_op jit(solution)/shard_map/reduce_scatter | solution.py:103
  621.0 33.2 %all_gather.34 = bf16[16,3,8192]{2,0,1:T(8,128)(2,1)S(1)} all-gather(bf16[16,3,512]{2,0,1:T(8,128)(2,1)} %reduce-scatter.20.cloned.1.call-done), channel_id=1, replica_groups=mesh['section'=2,'row'=16,'col'=8] {'row'}, dimensions={2}, use_global_device_ids=true | all-gather | bytes 835584 | tf_op jit(solution)/shard_map/all_gather | solution.py:114
  654.7 5.0 reduce-scatter.12.cloned.1.call-done
  659.7 33.2 %all_gather.29 = bf16[16,3,8192]{2,0,1:T(8,128)(2,1)S(1)} all-gather(bf16[16,3,512]{2,0,1:T(8,128)(2,1)} %reduce-scatter.12.cloned.1.call-done), channel_id=1, replica_groups=mesh['section'=2,'row'=16,'col'=8] {'row'}, dimensions={2}, use_global_device_ids=true | all-gather | bytes 835584 | tf_op jit(solution)/shard_map/all_gather | solution.py:113
  693.5 23.4 %all-gather.14.cloned.1.call-done = bf16[384,1792]{1,0:T(8,128)(2,1)} async-done(((bf16[24,1792]{1,0:T(8,128)(2,1)}), bf16[384,1792]{1,0:T(8,128)(2,1)}) %all-gather.14.cloned.1.call-update) | async-done | bytes 1376272 | tf_op jit(solution)/shard_map/all_gather | solution.py:88
  716.9 3.7 fusion.2
  720.6 3.8 copy.19
  724.4 3.8 copy.20
  (49 shorter events, 6.0 us)
Async XLA Ops:
  7.2 23.9 %copy-start = (bf16[1,512,1792]{2,1,0:T(8,128)(2,1)S(1)}, bf16[1,512,1792]{2,1,0:T(8,128)(2,1)}, u32[]{:S(2)}) copy-start(bf16[1,512,1792]{2,1,0:T(8,128)(2,1)} %param.10) | copy-start | bytes 5505028
  7.2 104.7 %reduce-scatter.16.cloned.1.call-start = ((), (), s32[]{:S(2)}) async-start(), calls=%async_computation.12 | async-start | bytes 1462272 | tf_op jit(solution)/shard_map/reduce_scatter | solution.py:78
  33.1 3.6 copy-start.1
  33.1 157.3 %reduce-scatter.18.cloned.1.call-start = ((), (), s32[]{:S(2)}) async-start(), calls=%async_computation.13 | async-start | bytes 1462272 | tf_op jit(solution)/shard_map/reduce_scatter | solution.py:75
  36.6 232.2 %reduce-scatter.14.cloned.1.call-start = ((), (), s32[]{:S(2)}) async-start(), calls=%async_computation.11 | async-start | bytes 1462272 | tf_op jit(solution)/shard_map/reduce_scatter | solution.py:81
  55.4 3.6 copy-start.2
  58.9 288.8 %reduce-scatter.10.cloned.1.call-start = ((), (), s32[]{:S(2)}) async-start(), calls=%async_computation.8 | async-start | bytes 1462272 | tf_op jit(solution)/shard_map/reduce_scatter | solution.py:72
  79.8 347.0 %reduce-scatter.8.cloned.1.call-start = ((), (), s32[]{:S(2)}) async-start(), calls=%async_computation.7 | async-start | bytes 1462272 | tf_op jit(solution)/shard_map/reduce_scatter | solution.py:69
  83.3 398.1 %all-gather.12.cloned.1.call-start = ((), (), s32[]{:S(2)}) async-start(), calls=%async_computation.15 | async-start | bytes 1462272 | tf_op jit(solution)/shard_map/all_gather | solution.py:90
  270.6 263.6 %all-gather.10.cloned.1.call-start = ((), (), s32[]{:S(2)}) async-start(), calls=%async_computation.14 | async-start | bytes 1462272 | tf_op jit(solution)/shard_map/all_gather | solution.py:89
  271.4 315.7 %all-gather.8.cloned.1.call-start = ((), (), s32[]{:S(2)}) async-start(), calls=%async_computation.9 | async-start | bytes 1462272 | tf_op jit(solution)/shard_map/all_gather | solution.py:87
  428.4 192.6 %reduce-scatter.20.cloned.1.call-start = ((), (), s32[]{:S(2)}) async-start(), calls=%async_computation.16 | async-start | bytes 442368 | tf_op jit(solution)/shard_map/reduce_scatter | solution.py:103
  538.4 51.5 %copy-start.3 = (bf16[1,48,512]{2,1,0:T(8,128)(2,1)S(1)}, bf16[1,48,512]{2,1,0:T(8,128)(2,1)}, u32[]{:S(2)}) copy-start(bf16[1,48,512]{2,1,0:T(8,128)(2,1)} %param.6) | copy-start | bytes 147460
  538.4 121.2 %reduce-scatter.12.cloned.1.call-start = ((), (), s32[]{:S(2)}) async-start(), calls=%async_computation.10 | async-start | bytes 442368 | tf_op jit(solution)/shard_map/reduce_scatter | solution.py:97
  591.3 125.6 %all-gather.14.cloned.1.call-start = ((), (), s32[]{:S(2)}) async-start(), calls=%async_computation.17 | async-start | bytes 1462272 | tf_op jit(solution)/shard_map/all_gather | solution.py:88
  592.0 3.8 copy-start.4
  654.3 73.9 %collective-permute-start.1 = (bf16[3,8192]{1,0:T(4,128)(2,1)S(1)}, bf16[3,8192]{1,0:T(4,128)(2,1)S(1)}, u32[]{:S(2)}, u32[]{:S(2)}) collective-permute-start(bf16[3,8192]{1,0:T(4,128)(2,1)S(1)} %bitcast.79), channel_id=1, source_target_pairs={{128,0},{0,128},{129,1},{1,129},{130,2},{2,130},{131,3},{3,131},{1... | collective-permute-start | bytes 147464 | tf_op jit(solution)/shard_map/ppermute | solution.py:10
  693.1 35.1 %collective-permute-start = (bf16[3,8192]{1,0:T(4,128)(2,1)S(1)}, bf16[3,8192]{1,0:T(4,128)(2,1)S(1)}, u32[]{:S(2)}, u32[]{:S(2)}) collective-permute-start(bf16[3,8192]{1,0:T(4,128)(2,1)S(1)} %bitcast.80), channel_id=1, source_target_pairs={{128,0},{0,128},{129,1},{1,129},{130,2},{2,130},{131,3},{3,131},{1... | collective-permute-start | bytes 147464 | tf_op jit(solution)/shard_map/ppermute | solution.py:10
Sparse Core Ops, SparseCore 0:
  33.2 78.5 reduce-scatter.15
  116.1 74.1 reduce-scatter.17
  194.6 74.1 reduce-scatter.13
  273.5 74.1 reduce-scatter.9
  352.5 74.2 reduce-scatter.7
  429.3 52.0 all-gather.11
  484.6 49.5 all-gather.9
  537.5 49.5 all-gather.7
  590.2 30.7 reduce-scatter.19
  624.0 35.5 reduce-scatter.11
  662.4 54.4 all-gather.13
where the time goes:
time: 737 us; the launch traced here: 736 us
  waiting for transfers between devices  546 us (74%)
  blocking collectives  128 us (17%)
  matrix products  32.2 us (4%)
  between operations  14 us (2%)
  local copies, waits for them, and re-layouts  11.7 us (2%)
    reduce_scatter x1, waiting for transfers between devices, body(): lax.psum_scatter(gate_new.astype(jnp.bfloat16), 'row', scatter_dimension=...  79 us
    reduce_scatter x1, waiting for transfers between devices, body(): lax.psum_scatter(gate_old.astype(jnp.bfloat16), 'row', scatter_dimension=...  78.5 us
    reduce_scatter x1, waiting for transfers between devices, body(): lax.psum_scatter(d_act.astype(jnp.bfloat16), 'row', scatter_dimension=0,...  78.5 us
    reduce_scatter x1, waiting for transfers between devices, body(): lax.psum_scatter(up_new.astype(jnp.bfloat16), 'row', scatter_dimension=0,...  76.4 us
    all_gather x1, waiting for transfers between devices, body(): lax.all_gather(local_parts[3], 'row', axis=0, tiled=True)  52.9 us
    all_gather x1, waiting for transfers between devices, body(): lax.all_gather(local_parts[2], 'row', axis=0, tiled=True)  50.6 us
    all_gather x1, waiting for transfers between devices, body(): lax.all_gather(local_parts[0], 'row', axis=0, tiled=True)  48.6 us
    all_gather x1, blocking collectives, body(): lax.all_gather(layer_out, 'row', axis=2, tiled=True)  33.2 us
  transfers between devices with their start and end apart: 13, of which 11 were waited for; matrix products, arithmetic and copies ran while one was open for 6% of the time, Pallas kernels for 0%

commit v1 on v0

v1 whole, which is shorter than its diff:
```python
import functools

import jax
import jax.numpy as jnp
from jax import lax
from jax.experimental import pallas as pl
from jax.experimental.pallas import tpu as pltpu
from jax.sharding import PartitionSpec as P

MESH = pl.DeviceIdType.MESH
BF = jnp.bfloat16
F32 = jnp.float32
T = 384
B = 48
DW = 512
H = 896


def dot(left, right):
    return lax.dot_general(left, right, (((1,), (0,)), ((), ())), preferred_element_type=F32)


def dot_nt(left, right):
    return lax.dot_general(left, right, (((1,), (1,)), ((), ())), preferred_element_type=F32)


def tiles(width, step, body):
    whole = width // step

    @pl.loop(0, whole)
    def _(i):
        body(pl.ds(pl.multiple_of(i * step, step), step))

    if width % step:
        body(pl.ds(whole * step, width % step))


def kernel(
    x_new, x_old, x_cot, wg, wu, wd,
    o_next, o_grad, o_gg, o_gu, o_gd,
    G, WgH, WuH, WdH, WgX, WuX, WdX,
    PS, RL, PL, AD, AR, KS, XS, XR,
    A, TT, OP, ZS, RP, RM, LC, ES, ED, PM, ST, GG, GD,
    wsem, zr_s, zr_r, zl_s, zl_r, gs_s, gs_r, wx_s, wx_r,
    rs_s, rs_r, cy_s, cy_r, cr_s, cr_r, cx_s, cx_r, cs_s, cs_r,
    dp_s, dp_r, dm_s, dm_r, e_s, e_r, osem,
):
    s = lax.axis_index("section")
    r = lax.axis_index("row")
    c = lax.axis_index("col")
    y, xh, k = r // 4, (r // 2) % 2, r % 2
    xo = 1 - xh
    q = y * 2 + xh
    sib = {"row": r + 1 - 2 * k}
    yp = {"row": ((y + 1) % 4) * 4 + xh * 2 + k}
    ym = {"row": ((y + 3) % 4) * 4 + xh * 2 + k}
    xp = {"row": y * 4 + xo * 2 + k}
    zp = {"col": (c + 1) % 8}
    zm = {"col": (c + 7) % 8}
    far = [{"section": 1 - s, "row": (r + j) % 16} for j in range(16)]

    barrier = pltpu.get_barrier_semaphore()
    partners = [sib, yp, ym, xp, zp, zm] + far
    for d in partners:
        pl.semaphore_signal(barrier, inc=1, device_id=d, device_id_type=MESH)

    mine = pl.multiple_of(k * H, 128)
    other = pl.multiple_of((1 - k) * H, 128)
    loads = []

    def load(src, dst):
        cp = pltpu.make_async_copy(src, dst, wsem.at[len(loads)])
        cp.start()
        loads.append(cp)

    load(wg.at[:, pl.ds(mine, H)], WgH.at[0])
    load(wu.at[:, pl.ds(mine, H)], WuH.at[0])
    load(wd.at[pl.ds(mine, H), :], WdH.at[0])
    load(wg.at[:, pl.ds(other, H)], WgH.at[1])
    load(wu.at[:, pl.ds(other, H)], WuH.at[1])
    load(wd.at[pl.ds(other, H), :], WdH.at[1])

    def rows(block):
        return pl.ds(pl.multiple_of(lax.rem(block + 16, 8) * B, 16), B)

    sent = []

    def send(src, dst, ssem, rsem, to):
        cp = pltpu.make_async_remote_copy(
            src_ref=src, dst_ref=dst, send_sem=ssem, recv_sem=rsem, device_id=to, device_id_type=MESH
        )
        cp.start()
        sent.append(cp)
        return cp

    def got(ref, ssem, rsem):
        pltpu.make_async_remote_copy(
            src_ref=ref, dst_ref=ref, send_sem=ssem, recv_sem=rsem, device_id=sib, device_id_type=MESH
        ).wait_recv()

    xs = (x_new, x_old, x_cot)
    for a in range(3):
        G[a, 0, rows(c), :] = xs[a][...]

    pl.semaphore_wait(barrier, len(partners))

    hops_r = (4, 3, 4)
    hops_l = (3, 4, 3)

    def z_right(a, i):
        ref = G.at[a, 0, rows(c - i), :]
        send(ref, ref, zr_s.at[a, i], zr_r.at[a, i], zp)

    def z_left(a, i):
        ref = G.at[a, 0, rows(c + i), :]
        send(ref, ref, zl_s.at[a, i], zl_r.at[a, i], zm)

    def z_step(a, i):
        if i < hops_r[a]:
            if i > 0:
                got(G.at[a, 0, rows(c - i), :], zr_s.at[a, i - 1], zr_r.at[a, i - 1])
            z_right(a, i)
        elif i == hops_r[a]:
            got(G.at[a, 0, rows(c - i), :], zr_s.at[a, i - 1], zr_r.at[a, i - 1])
        if i < hops_l[a]:
            if i > 0:
                got(G.at[a, 0, rows(c + i), :], zl_s.at[a, i - 1], zl_r.at[a, i - 1])
            z_left(a, i)
        elif i == hops_l[a]:
            got(G.at[a, 0, rows(c + i), :], zl_s.at[a, i - 1], zl_r.at[a, i - 1])

    def z_share(a):
        send(G.at[a, 0], G.at[a, 1], gs_s.at[a], gs_r.at[a], sib)

    def z_shared(a):
        got(G.at[a, 1], gs_s.at[a], gs_r.at[a])

    def stage1(a, w):
        if a == 4:
            def tile(cols):
                acc = dot_nt(G[2, 0], WdH[0, cols, :]) + dot_nt(G[2, 1], WdX[cols, :])
                PS[a, :, cols] = acc.astype(BF)
        else:
            own, theirs = ((WgH, WgX), (WuH, WuX))[a % 2]
            t = a // 2

            def tile(cols):
                acc = dot(G[t, 0], own[0, :, cols]) + dot(G[t, 1], theirs[:, cols])
                PS[a, :, cols] = acc.astype(BF)

        tiles(H, 256, tile)
        up, down, across = 2 * (y + 1), 2 * (y - 1), 2 * (y + 2)
        send(PS.at[a, rows(across), :], RL.at[a, 0], rs_s.at[a, 0], rs_r.at[a, 0], yp)
        send(PS.at[a, rows(across + 1), :], RL.at[a, 1], rs_s.at[a, 1], rs_r.at[a, 1], ym)
        send(PS.at[a, rows(up + 1), :], PL.at[a, 1], rs_s.at[a, 2], rs_r.at[a, 2], yp)
        send(PS.at[a, rows(down), :], PL.at[a, 0], rs_s.at[a, 3], rs_r.at[a, 3], ym)

    def stage2(a):
        up, down = 2 * (y + 1), 2 * (y - 1)
        got(RL.at[a, 0], rs_s.at[a, 0], rs_r.at[a, 0])
        AD[a, 0] = (PS[a, rows(up), :].astype(F32) + RL[a, 0].astype(F32)).astype(BF)
        send(AD.at[a, 0], AR.at[a, 0], rs_s.at[a, 4], rs_r.at[a, 4], yp)
        got(RL.at[a, 1], rs_s.at[a, 1], rs_r.at[a, 1])
        AD[a, 1] = (PS[a, rows(down + 1), :].astype(F32) + RL[a, 1].astype(F32)).astype(BF)
        send(AD.at[a, 1], AR.at[a, 1], rs_s.at[a, 5], rs_r.at[a, 5], ym)

    def stage3(a):
        got(PL.at[a, 1], rs_s.at[a, 2], rs_r.at[a, 2])
        got(PL.at[a, 0], rs_s.at[a, 3], rs_r.at[a, 3])
        got(AR.at[a, 0], rs_s.at[a, 4], rs_r.at[a, 4])
        got(AR.at[a, 1], rs_s.at[a, 5], rs_r.at[a, 5])

        def total(which):
            return (
                PS[a, rows(2 * y + which), :].astype(F32)
                + PL[a, which].astype(F32)
                + AR[a, which].astype(F32)
            )

        XS[a] = total(xo).astype(BF)
        send(XS.at[a], XR.at[a], rs_s.at[a, 6], rs_r.at[a, 6], xp)
        KS[a] = total(xh)

    def stage4(a):
        got(XR.at[a], rs_s.at[a, 6], rs_r.at[a, 6])

    def value(a, cols):
        return KS[a, :, cols] + XR[a, :, cols].astype(F32)

    def sigmoid(v):
        return 1.0 / (1.0 + jnp.exp(-v))

    def activate_new():
        def tile(cols):
            gate, up = value(0, cols), value(1, cols)
            A[0, 0, rows(q), cols] = (gate * sigmoid(gate) * up).astype(BF)

        tiles(H, 128, tile)

    def activate_old():
        def tile(cols):
            gate, up, d = value(2, cols), value(3, cols), value(4, cols)
            sg = sigmoid(gate)
            A[1, 0, rows(q), cols] = (d * up * sg * (1.0 + gate * (1.0 - sg))).astype(BF)
            A[2, 0, rows(q), cols] = (d * gate * sg).astype(BF)
            A[3, 0, rows(q), cols] = (gate * sg * up).astype(BF)

        tiles(H, 128, tile)

    def c1(b):
        ref = A.at[b, 0, rows(q), :]
        send(ref, ref, cx_s.at[b], cx_r.at[b], xp)
        send(ref, ref, cy_s.at[b, 0, xh], cy_r.at[b, 0, xh], yp)
        send(ref, ref, cy_s.at[b, 1, xh], cy_r.at[b, 1, xh], ym)

    def c2(b):
        ref = A.at[b, 0, rows(2 * y + xo), :]
        got(ref, cx_s.at[b], cx_r.at[b])
        send(ref, ref, cy_s.at[b, 0, xo], cy_r.at[b, 0, xo], yp)
        send(ref, ref, cy_s.at[b, 1, xo], cy_r.at[b, 1, xo], ym)

    def c3(b):
        ref = A.at[b, 0, rows(2 * (y - 1)), :]
        got(ref, cy_s.at[b, 0, 0], cy_r.at[b, 0, 0])
        send(ref, ref, cr_s.at[b, 0], cr_r.at[b, 0], yp)
        ref = A.at[b, 0, rows(2 * (y + 1) + 1), :]
        got(ref, cy_s.at[b, 1, 1], cy_r.at[b, 1, 1])
        send(ref, ref, cr_s.at[b, 1], cr_r.at[b, 1], ym)

    def c4(b):
        got(A.at[b, 0, rows(2 * (y - 1) + 1), :], cy_s.at[b, 0, 1], cy_r.at[b, 0, 1])
        got(A.at[b, 0, rows(2 * (y + 1)), :], cy_s.at[b, 1, 0], cy_r.at[b, 1, 0])
        got(A.at[b, 0, rows(2 * (y + 2)), :], cr_s.at[b, 0], cr_r.at[b, 0])
        got(A.at[b, 0, rows(2 * (y + 2) + 1), :], cr_s.at[b, 1], cr_r.at[b, 1])
        send(A.at[b, 0], A.at[b, 1], cs_s.at[b], cs_r.at[b], sib)

    def c5(b):
        got(A.at[b, 1], cs_s.at[b], cs_r.at[b])

    def part_out():
        def tile(cols):
            acc = dot(A[0, 0], WdH[0, :, cols]) + dot(A[0, 1], WdH[1, :, cols])
            TT[0, :, cols] = acc.astype(BF)

        tiles(DW, 256, tile)

    def part_grad():
        def tile(cols):
            acc = dot_nt(A[1, 0], WgH[0, cols, :]) + dot_nt(A[1, 1], WgH[1, cols, :])
            acc += dot_nt(A[2, 0], WuH[0, cols, :]) + dot_nt(A[2, 1], WuH[1, cols, :])
            TT[1, :, cols] = acc.astype(BF)

        tiles(DW, 256, tile)

    hops_p = (4, 3)
    hops_m = (3, 4)

    def z_order(e):
        def tile(cols):
            OP[e, :, cols] = dot(PM[...], TT[e, :, cols]).astype(BF)

        tiles(DW, 256, tile)

    def d_step(e, i):
        for n, sem_s, sem_r, land, to, sign, side in (
            (hops_p[e], dp_s, dp_r, RP, zp, 1, 0),
            (hops_m[e], dm_s, dm_r, RM, zm, -1, 1),
        ):
            if i >= n:
                continue
            here = rows(c + sign * (n - i))
            if i == 0:
                send(OP.at[e, here, :], land.at[e, i], sem_s.at[e, i], sem_r.at[e, i], to)
            else:
                got(land.at[e, i - 1], sem_s.at[e, i - 1], sem_r.at[e, i - 1])
                ZS[e, side, i - 1] = (
                    OP[e, here, :].astype(F32) + land[e, i - 1].astype(F32)
                ).astype(BF)
                send(ZS.at[e, side, i - 1], land.at[e, i], sem_s.at[e, i], sem_r.at[e, i], to)

    def d_last(e):
        n, m = hops_p[e], hops_m[e]
        got(RP.at[e, n - 1], dp_s.at[e, n - 1], dp_r.at[e, n - 1])
        got(RM.at[e, m - 1], dm_s.at[e, m - 1], dm_r.at[e, m - 1])
        kept = dot(PM[rows(c), :], G[0 if e == 0 else 2, 0])
        full = OP[e, rows(c), :].astype(F32) + RP[e, n - 1].astype(F32) + RM[e, m - 1].astype(F32)
        LC[e * B : (e + 1) * B, :] = (full + kept).astype(BF)

    outs = []

    def put(src, dst):
        cp = pltpu.make_async_copy(src, dst, osem.at[len(outs)])
        cp.start()
        outs.append(cp)

    def grad_in(b, h):
        def tile(cols):
            GG[b - 1, h, :, cols] = dot(ST[...], A[b, h, :, cols]).astype(BF)

        tiles(H, 256, tile)
        put(GG.at[b - 1, h], (o_gg, o_gu)[b - 1].at[:, pl.ds((mine, other)[h], H)])

    def grad_out(h):
        def tile(cols):
            GD[h, cols, :] = lax.dot_general(
                A[3, h, :, cols], G[2, 0], (((0,), (0,)), ((), ())), preferred_element_type=F32
            ).astype(BF)

        tiles(H, 256, tile)
        put(GD.at[h], o_gd.at[pl.ds((mine, other)[h], H), :])

    send(wg.at[:, pl.ds(other, H)], WgX, wx_s.at[0], wx_r.at[0], sib)
    send(wu.at[:, pl.ds(other, H)], WuX, wx_s.at[1], wx_r.at[1], sib)
    send(wd.at[pl.ds(other, H), :], WdX, wx_s.at[2], wx_r.at[2], sib)

    z_step(0, 0)
    z_step(0, 1)
    z_step(1, 0)
    z_step(0, 2)
    z_step(1, 1)
    z_step(0, 3)
    z_step(2, 0)
    z_step(0, 4)
    z_share(0)
    z_step(1, 2)
    z_step(2, 1)

    pi = lax.broadcasted_iota(jnp.int32, (T, T), 0)
    ti = lax.broadcasted_iota(jnp.int32, (T, T), 1)
    token = ((pi % B) // 3) * 24 + (pi // B) * 3 + pi % 3
    PM[...] = jnp.where(ti == token, 1.0, 0.0).astype(BF)

    for cp in loads[:3]:
        cp.wait()
    got(WgX, wx_s.at[0], wx_r.at[0])
    got(WuX, wx_s.at[1], wx_r.at[1])
    z_shared(0)
    stage1(0, 0)
    z_step(1, 3)
    z_step(2, 2)
    stage1(1, 0)
    z_step(1, 4)
    z_share(1)
    z_step(2, 3)
    stage2(0)
    z_step(2, 4)
    z_share(2)
    z_shared(1)
    stage1(2, 0)
    stage2(1)
    stage3(0)
    stage1(3, 0)
    stage2(2)
    stage3(1)
    stage4(0)
    got(WdX, wx_s.at[2], wx_r.at[2])
    z_shared(2)
    stage1(4, 0)
    stage4(1)
    activate_new()
    stage2(3)
    c1(0)
    stage3(2)
    stage2(4)
    c2(0)
    stage3(3)
    c3(0)
    stage4(2)
    stage3(4)
    ST[...] = jnp.transpose(G[1, 0])
    stage4(3)
    c4(0)
    stage4(4)
    activate_old()
    c1(1)
    c1(2)
    c2(1)
    c2(2)
    for cp in loads[3:]:
        cp.wait()
    c5(0)
    part_out()
    z_order(0)
    d_step(0, 0)
    c3(1)
    c3(2)
    c1(3)
    d_step(0, 1)
    c4(1)
    d_step(0, 2)
    c4(2)
    c2(3)
    c5(1)
    c5(2)
    part_grad()
    z_order(1)
    d_step(1, 0)
    c3(3)
    d_step(0, 3)
    grad_in(1, 0)
    d_step(1, 1)
    c4(3)
    grad_in(1, 1)
    d_last(0)
    d_step(1, 2)
    grad_in(2, 0)
    d_step(1, 3)
    grad_in(2, 1)
    d_last(1)

    ri = lax.broadcasted_iota(jnp.int32, (256, 2 * B), 0)
    li = lax.broadcasted_iota(jnp.int32, (256, 2 * B), 1)
    sub = ri % 8
    spread = jnp.where((sub < 3) & (li == ((ri % 16) // 8) * B + (ri // 16) * 3 + sub), 1.0, 0.0)
    ES[...] = dot(spread.astype(BF), LC[...]).astype(BF)
    for j in range(16):
        there = pl.ds(pl.multiple_of(((r + j) % 16) * 16, 16), 16)
        here = pl.ds(pl.multiple_of(r * 16, 16), 16)
        send(ES.at[there, :], ED.at[here, :], e_s.at[j], e_r.at[j], far[j])

    c5(3)
    grad_out(0)
    grad_out(1)
    for j in range(16):
        got(ED.at[pl.ds(pl.multiple_of(((r + 16 - j) % 16) * 16, 16), 16), :], e_s.at[j], e_r.at[j])
    for j in range(16):
        tile = ED[j * 16 : j * 16 + 16, :]
        o_next[:, j * DW : (j + 1) * DW] = tile[0:3]
        o_grad[:, j * DW : (j + 1) * DW] = tile[8:11]
    for cp in outs:
        cp.wait()
    for cp in sent:
        cp.wait_send()


def body(fwd_in, bwd_in, cotangent, w_gate, w_up, w_down):
    vmem = pl.BlockSpec(memory_space=pltpu.VMEM)
    hbm = pl.BlockSpec(memory_space=pl.ANY)
    V = pltpu.VMEM
    D = pltpu.SemaphoreType.DMA
    scratch = [
        V((3, 2, T, DW), BF),
        V((2, DW, H), BF), V((2, DW, H), BF), V((2, H, DW), BF),
        V((DW, H), BF), V((DW, H), BF), V((H, DW), BF),
        V((5, T, H), BF),
        V((5, 2, B, H), BF), V((5, 2, B, H), BF), V((5, 2, B, H), BF), V((5, 2, B, H), BF),
        V((5, B, H), F32), V((5, B, H), BF), V((5, B, H), BF),
        V((4, 2, T, H), BF),
        V((2, T, DW), BF), V((2, T, DW), BF),
        V((2, 2, 3, B, DW), BF), V((2, 4, B, DW), BF), V((2, 4, B, DW), BF),
        V((2 * B, DW), BF), V((256, DW), BF), V((256, DW), BF),
        V((T, T), BF), V((DW, T), BF),
        V((2, 2, DW, H), BF), V((2, H, DW), BF),
        D((6,)), D((3, 4)), D((3, 4)), D((3, 4)), D((3, 4)), D((3,)), D((3,)), D((3,)), D((3,)),
        D((5, 7)), D((5, 7)), D((4, 2, 2)), D((4, 2, 2)), D((4, 2)), D((4, 2)),
        D((4,)), D((4,)), D((4,)), D((4,)),
        D((2, 4)), D((2, 4)), D((2, 4)), D((2, 4)), D((16,)), D((16,)), D((6,)),
    ]
    n, g, gg, gu, gd = pl.pallas_call(
        kernel,
        out_shape=(
            jax.ShapeDtypeStruct((3, 16 * DW), BF),
            jax.ShapeDtypeStruct((3, 16 * DW), BF),
            jax.ShapeDtypeStruct((DW, 2 * H), BF),
            jax.ShapeDtypeStruct((DW, 2 * H), BF),
            jax.ShapeDtypeStruct((2 * H, DW), BF),
        ),
        in_specs=[vmem] * 3 + [hbm] * 3,
        out_specs=(vmem, vmem, hbm, hbm, hbm),
        scratch_shapes=scratch,
        compiler_params=pltpu.CompilerParams(
            collective_id=0, has_side_effects=True, vmem_limit_bytes=56 * 2**20
        ),
        cost_estimate=pl.CostEstimate(flops=8 * 10**9, bytes_accessed=12 * 10**6, transcendentals=0),
        name="relay",
    )(fwd_in[0], bwd_in[0], cotangent[0], w_gate[0], w_up[0], w_down[0])
    return n[None], g[None], gg[None], gu[None], gd[None]


def solution(mesh):
    in_specs = (
        P("section", "col", "row"),
        P("section", "col", "row"),
        P("section", "col", "row"),
        P("section", "row", "col"),
        P("section", "row", "col"),
        P("section", "col", "row"),
    )
    out_specs = (
        P("section", ("row", "col"), None),
        P("section", ("row", "col"), None),
        P("section", "row", "col"),
        P("section", "row", "col"),
        P("section", "col", "row"),
    )
    return jax.shard_map(body, mesh=mesh, in_specs=in_specs, out_specs=out_specs, check_vma=False)
```

time: 737 us -> 116 us (0.16)
  waiting for transfers between devices: 546 us -> 0 us
  blocking collectives: 128 us -> 0 us
  Pallas kernels: 0 us -> 106 us
  matrix products: 32.2 us -> 0 us
  between operations: 14 us -> 0.65 us
    reduce_scatter x7 -> x0, waiting for transfers between devices: 369 us -> none  [the longest x1 79 us: body(): lax.psum_scatter(gate_new.astype(jnp.bfloat16), 'row', scatter_dimension=...]
    all_gather x4 -> x0, waiting for transfers between devices: 176 us -> none  [the longest x1 52.9 us: body(): lax.all_gather(local_parts[3], 'row', axis=0, tiled=True)]
    all_gather x5 -> x0, blocking collectives: 128 us -> none  [the longest x1 33.2 us: body(): lax.all_gather(layer_out, 'row', axis=2, tiled=True)]
    pallas_call x0 -> x1, Pallas kernels: none -> 106 us  [body(): pl.pallas_call(kernel, out_shape=(jax.ShapeDtypeStruct((3, 16 * DW), BF),...]
    dot_general x11 -> x0, matrix products: 32.2 us -> none  [the longest x6 18.5 us: against(): lax.dot_general(left, right, (((dims[0],), (dims[1],)), ((), ())), prefer...]
  transfers between devices with their start and end apart: 13 -> 0, of which waited for: 11 -> 0; matrix products, arithmetic and copies ran while one was open for 6% -> 0% of each run, Pallas kernels for 0% -> 0%
where the time goes in v1:
time: 116 us
  Pallas kernels  106 us (91%)
  local copies, waits for them, and re-layouts  9.36 us (8%)
    pallas_call x1, Pallas kernels, body(): pl.pallas_call(kernel, out_shape=(jax.ShapeDtypeStruct((3, 16 * DW), BF),...  106 us
    unnamed x9, local copies, waits for them, and re-layouts  9.36 us

profile of v1, /device:TPU:1, one launch (start us, length us, event | category | flops | bytes accessed | tf_op | source)
XLA Modules:
  0.0 115.7 jit_solution(15719086251864882630)
XLA Ops:
  0.6 105.7 %relay.1 = (bf16[3,8192]{1,0:T(4,128)(2,1)}, bf16[3,8192]{1,0:T(4,128)(2,1)}, bf16[512,1792]{1,0:T(8,128)(2,1)}, bf16[512,1792]{1,0:T(8,128)(2,1)}, bf16[1792,512]{1,0:T(8,128)(2,1)}) custom-call(bf16[48,512]{1,0:T(8,128)(2,1)} %bitcast.19, bf16[48,512]{1,0:T(8,128)(2,1)} %bitcast.20, bf16[48,512]{1,0:T(8,128)(2,1)} %bitcast.21, bf16[512,1792]{1,0:T(8,128)(2,1)} %bitcast.16, ...), custom_call_target="tpu_custom_call" | custom-call | flops 8000000000 | bytes 12000000 | tf_op jit(solution)/shard_map/relay/pallas_call | solution.py:459
  106.4 1.5 %copy.16 = bf16[1,3,8192]{2,1,0:T(4,128)(2,1)} copy(bf16[1,3,8192]{2,1,0:T(4,128)(2,1)} %bitcast.15) | data formatting | bytes 98304
  107.9 1.5 %copy.17 = bf16[1,3,8192]{2,1,0:T(4,128)(2,1)} copy(bf16[1,3,8192]{2,1,0:T(4,128)(2,1)} %bitcast.14) | data formatting | bytes 98304
  109.4 0.0 copy-start.1
  109.4 3.0 %copy.18 = bf16[1,512,1792]{2,1,0:T(8,128)(2,1)} copy(bf16[1,512,1792]{2,1,0:T(8,128)(2,1)} %bitcast.13) | data formatting | bytes 3670016
  112.4 0.0 copy-done.1
  112.4 0.0 copy-start
  112.4 1.2 %copy.19 = bf16[1,512,1792]{2,1,0:T(8,128)(2,1)} copy(bf16[1,512,1792]{2,1,0:T(8,128)(2,1)S(1)} %bitcast.12) | data formatting | bytes 3670016
  113.6 0.9 copy-done
  114.5 1.2 %copy.20 = bf16[1,1792,512]{2,1,0:T(8,128)(2,1)} copy(bf16[1,1792,512]{2,1,0:T(8,128)(2,1)S(1)} %bitcast.11) | data formatting | bytes 3670016
Async XLA Ops:
  109.4 3.0 %copy-start.1 = (bf16[512,1792]{1,0:T(8,128)(2,1)S(1)}, bf16[512,1792]{1,0:T(8,128)(2,1)}, u32[]{:S(2)}) copy-start(bf16[512,1792]{1,0:T(8,128)(2,1)} %get-tuple-element.13) | copy-start | bytes 5505028
  112.4 2.2 %copy-start = (bf16[1792,512]{1,0:T(8,128)(2,1)S(1)}, bf16[1792,512]{1,0:T(8,128)(2,1)}, u32[]{:S(2)}) copy-start(bf16[1792,512]{1,0:T(8,128)(2,1)} %get-tuple-element.14) | copy-start | bytes 5505028

commit v2 on v1

v2 whole, which is shorter than its diff:
```python
import functools

import jax
import jax.numpy as jnp
from jax import lax
from jax.experimental import pallas as pl
from jax.experimental.pallas import tpu as pltpu
from jax.sharding import PartitionSpec as P

MESH = pl.DeviceIdType.MESH
BF = jnp.bfloat16
F32 = jnp.float32
T = 384
B = 48
DW = 512
H = 896
LOW, HIGH = pl.ds(0, 512), pl.ds(512, 384)
SUM_X = {1: 0, 3: 1}
GATHER_X = (2, 3)


def dot(left, right):
    return lax.dot_general(left, right, (((1,), (0,)), ((), ())), preferred_element_type=F32)


def dot_nt(left, right):
    return lax.dot_general(left, right, (((1,), (1,)), ((), ())), preferred_element_type=F32)


def tiles(width, step, body):
    whole = width // step

    @pl.loop(0, whole)
    def _(i):
        body(pl.ds(pl.multiple_of(i * step, step), step))

    if width % step:
        body(pl.ds(whole * step, width % step))


def kernel(
    x_new, x_old, x_cot, wg, wu, wd,
    o_seen, o_gg, o_gu, o_gd,
    G, WgH, WuH, WdH, WgX, WuX, WdX,
    PS, RL, PL, AD, AR, KS, XS, XR, XQ, SX,
    A, TT, AC, OP, ZS, RD, RES, LS, ES, ED, PM, SP, ST, GG, GD,
    wsem, xsem, z_s, z_r, gs_s, gs_r, wx_s, wx_r,
    rs_s, rs_r, cy_s, cy_r, cr_s, cr_r, cx_s, cx_r, cs_s, cs_r,
    d_s, d_r, e_s, e_r, osem, row_sem,
):
    s = lax.axis_index("section")
    r = lax.axis_index("row")
    c = lax.axis_index("col")
    y, xh, k = r // 4, (r // 2) % 2, r % 2
    xo = 1 - xh
    q = y * 2 + xh
    sib = {"row": r + 1 - 2 * k}
    yp = {"row": ((y + 1) % 4) * 4 + xh * 2 + k}
    ym = {"row": ((y + 3) % 4) * 4 + xh * 2 + k}
    xp = {"row": y * 4 + xo * 2 + k}
    zat = {d: {"col": (c + d + 8) % 8} for d in (1, -1, 2, -2)}
    far = [{"section": 1 - s, "row": (r + j) % 16} for j in range(16)]

    barrier = pltpu.get_barrier_semaphore()
    partners = [sib, yp, ym, xp, {"section": 1 - s}] + list(zat.values())
    for d in partners:
        pl.semaphore_signal(barrier, inc=1, device_id=d, device_id_type=MESH)

    mine = pl.multiple_of(k * H, 128)
    other = pl.multiple_of((1 - k) * H, 128)
    loads = []

    def load(src, dst):
        cp = pltpu.make_async_copy(src, dst, wsem.at[len(loads)])
        cp.start()
        loads.append(cp)

    def load_early():
        load(wg.at[:, pl.ds(mine, H)], WgH.at[0])
        load(wu.at[:, pl.ds(mine, H)], WuH.at[0])

    def load_down():
        load(wd.at[pl.ds(mine, H), :], WdH.at[0])
        send(wd.at[pl.ds(other, H), :], WdX, wx_s.at[2], wx_r.at[2], sib)

    def load_late():
        load(wg.at[:, pl.ds(other, H)], WgH.at[1])
        load(wu.at[:, pl.ds(other, H)], WuH.at[1])
        load(wd.at[pl.ds(other, H), :], WdH.at[1])

    def rows(block):
        return pl.ds(pl.multiple_of(lax.rem(block + 16, 8) * B, 16), B)

    sent = []

    def send(src, dst, ssem, rsem, to):
        cp = pltpu.make_async_remote_copy(
            src_ref=src, dst_ref=dst, send_sem=ssem, recv_sem=rsem, device_id=to, device_id_type=MESH
        )
        cp.start()
        sent.append(cp)
        return cp

    def got(ref, ssem, rsem):
        pltpu.make_async_remote_copy(
            src_ref=ref, dst_ref=ref, send_sem=ssem, recv_sem=rsem, device_id=sib, device_id_type=MESH
        ).wait_recv()

    xs = (x_new, x_old, x_cot)
    kept = []
    for a in range(3):
        cp = pltpu.make_async_copy(xs[a], G.at[a, 0, rows(c), :], xsem.at[a])
        cp.start()
        kept.append(cp)
    load_early()
    pl.semaphore_wait(barrier, len(partners))

    def z_send(a, src, block, j, to):
        ref = G.at[a, 0, rows(block), :]
        send(ref if src is None else src, ref, z_s.at[a, j], z_r.at[a, j], zat[to])

    def z_got(a, block, j):
        ref = G.at[a, 0, rows(block), :]
        got(ref, z_s.at[a, j], z_r.at[a, j])
        send(ref, G.at[a, 1, rows(block), :], gs_s.at[a, j], gs_r.at[a, j], sib)

    def z1(a):
        z_send(a, xs[a], c, 2, 2)
        z_send(a, xs[a], c, 3, -2)
        z_send(a, xs[a], c, 0, 1)
        z_send(a, xs[a], c, 1, -1)
        send(xs[a], G.at[a, 1, rows(c), :], gs_s.at[a, 7], gs_r.at[a, 7], sib)

    def z_near(a):
        z_got(a, c - 1, 0)
        z_got(a, c + 1, 1)

    def z2(a):
        z_got(a, c - 2, 2)
        if a % 2 == 0:
            z_send(a, None, c - 2, 6, 2)
        z_send(a, None, c - 2, 4, 1)
        z_got(a, c + 2, 3)
        if a % 2 == 1:
            z_send(a, None, c + 2, 6, -2)
        z_send(a, None, c + 2, 5, -1)

    def z3(a):
        z_got(a, c - 3, 4)
        z_got(a, c + 3, 5)
        z_got(a, c + 4, 6)

    def z_shared(a):
        kept[a].wait()
        for j in range(8):
            got(G.at[a, 1, rows(c), :], gs_s.at[a, j], gs_r.at[a, j])

    def stage1(a):
        if a == 4:
            def tile(cols):
                acc = dot_nt(G[2, 0], WdH[0, cols, :]) + dot_nt(G[2, 1], WdX[cols, :])
                PS[a, :, cols] = acc.astype(BF)
        else:
            own, theirs = ((WgH, WgX), (WuH, WuX))[a % 2]
            t = a // 2

            def tile(cols):
                acc = dot(G[t, 0], own[0, :, cols]) + dot(G[t, 1], theirs[:, cols])
                PS[a, :, cols] = acc.astype(BF)

        tiles(H, 256, tile)
        up, down, across = 2 * (y + 1), 2 * (y - 1), 2 * (y + 2)
        if a in SUM_X:
            for j, block in enumerate((across, up, down, 2 * y)):
                send(PS.at[a, rows(block + xo), :], XQ.at[SUM_X[a], j], rs_s.at[a, j], rs_r.at[a, j], xp)
            return
        send(PS.at[a, rows(across), :], RL.at[a, 0], rs_s.at[a, 0], rs_r.at[a, 0], yp)
        send(PS.at[a, rows(across + 1), :], RL.at[a, 1], rs_s.at[a, 1], rs_r.at[a, 1], ym)
        send(PS.at[a, rows(up + 1), :], PL.at[a, 1], rs_s.at[a, 2], rs_r.at[a, 2], yp)
        send(PS.at[a, rows(down), :], PL.at[a, 0], rs_s.at[a, 3], rs_r.at[a, 3], ym)

    def crossed(a, j, block):
        return PS[a, rows(block + xh), :].astype(F32) + XQ[SUM_X[a], j].astype(F32)

    def stage2x(a):
        n = SUM_X[a]
        got(XQ.at[n, 0], rs_s.at[a, 0], rs_r.at[a, 0])
        SX[n, 0] = crossed(a, 0, 2 * (y + 2)).astype(BF)
        send(SX.at[n, 0, :, LOW], RL.at[a, 0, :, LOW], rs_s.at[a, 4], rs_r.at[a, 4], yp)
        send(SX.at[n, 0, :, HIGH], RL.at[a, 0, :, HIGH], rs_s.at[a, 5], rs_r.at[a, 5], ym)
        got(XQ.at[n, 1], rs_s.at[a, 1], rs_r.at[a, 1])
        SX[n, 1] = crossed(a, 1, 2 * (y + 1)).astype(BF)
        send(SX.at[n, 1, :, HIGH], PL.at[a, 0, :, HIGH], rs_s.at[a, 6], rs_r.at[a, 6], yp)
        got(XQ.at[n, 2], rs_s.at[a, 2], rs_r.at[a, 2])
        SX[n, 2] = crossed(a, 2, 2 * (y - 1)).astype(BF)
        send(SX.at[n, 2, :, LOW], PL.at[a, 0, :, LOW], rs_s.at[a, 7], rs_r.at[a, 7], ym)
        got(XQ.at[n, 3], rs_s.at[a, 3], rs_r.at[a, 3])
        KS[a] = crossed(a, 3, 2 * y)

    def stage3x(a):
        n = SUM_X[a]
        got(RL.at[a, 0, :, LOW], rs_s.at[a, 4], rs_r.at[a, 4])
        full = PS[a, rows(2 * (y + 1) + xh), LOW].astype(F32) + XQ[n, 1, :, LOW].astype(F32)
        AD[a, 0, :, LOW] = (full + RL[a, 0, :, LOW].astype(F32)).astype(BF)
        send(AD.at[a, 0, :, LOW], AR.at[a, 0, :, LOW], rs_s.at[a, 8], rs_r.at[a, 8], yp)
        got(RL.at[a, 0, :, HIGH], rs_s.at[a, 5], rs_r.at[a, 5])
        full = PS[a, rows(2 * (y - 1) + xh), HIGH].astype(F32) + XQ[n, 2, :, HIGH].astype(F32)
        AD[a, 0, :, HIGH] = (full + RL[a, 0, :, HIGH].astype(F32)).astype(BF)
        send(AD.at[a, 0, :, HIGH], AR.at[a, 0, :, HIGH], rs_s.at[a, 9], rs_r.at[a, 9], ym)

    def stage4x(a):
        for j, cols in ((6, HIGH), (7, LOW), (8, LOW), (9, HIGH)):
            got(RL.at[a, 0, :, cols], rs_s.at[a, j], rs_r.at[a, j])

    def stage2(a):
        up, down = 2 * (y + 1), 2 * (y - 1)
        got(RL.at[a, 0], rs_s.at[a, 0], rs_r.at[a, 0])
        AD[a, 0] = (PS[a, rows(up), :].astype(F32) + RL[a, 0].astype(F32)).astype(BF)
        send(AD.at[a, 0], AR.at[a, 0], rs_s.at[a, 4], rs_r.at[a, 4], yp)
        got(RL.at[a, 1], rs_s.at[a, 1], rs_r.at[a, 1])
        AD[a, 1] = (PS[a, rows(down + 1), :].astype(F32) + RL[a, 1].astype(F32)).astype(BF)
        send(AD.at[a, 1], AR.at[a, 1], rs_s.at[a, 5], rs_r.at[a, 5], ym)

    def stage3(a):
        got(PL.at[a, 1], rs_s.at[a, 2], rs_r.at[a, 2])
        got(PL.at[a, 0], rs_s.at[a, 3], rs_r.at[a, 3])
        got(AR.at[a, 0], rs_s.at[a, 4], rs_r.at[a, 4])
        got(AR.at[a, 1], rs_s.at[a, 5], rs_r.at[a, 5])

        def total(which):
            return (
                PS[a, rows(2 * y + which), :].astype(F32)
                + PL[a, which].astype(F32)
                + AR[a, which].astype(F32)
            )

        XS[a] = total(xo).astype(BF)
        send(XS.at[a], XR.at[a], rs_s.at[a, 6], rs_r.at[a, 6], xp)
        KS[a] = total(xh)

    def stage4(a):
        got(XR.at[a], rs_s.at[a, 6], rs_r.at[a, 6])

    def value(a, cols):
        if a in SUM_X:
            return KS[a, :, cols] + PL[a, 0, :, cols].astype(F32) + AR[a, 0, :, cols].astype(F32)
        return KS[a, :, cols] + XR[a, :, cols].astype(F32)

    def sigmoid(v):
        return 1.0 / (1.0 + jnp.exp(-v))

    def activate_new():
        def tile(cols):
            gate, up = value(0, cols), value(1, cols)
            A[0, 0, rows(q), cols] = (gate * sigmoid(gate) * up).astype(BF)

        tiles(H, 128, tile)

    def activate_old():
        def tile(cols):
            gate, up, d = value(2, cols), value(3, cols), value(4, cols)
            sg = sigmoid(gate)
            A[1, 0, rows(q), cols] = (d * up * sg * (1.0 + gate * (1.0 - sg))).astype(BF)
            A[2, 0, rows(q), cols] = (d * gate * sg).astype(BF)
            A[3, 0, rows(q), cols] = (gate * sg * up).astype(BF)

        tiles(H, 128, tile)

    def share(b, ref, block, j):
        send(ref, A.at[b, 1, rows(block), :], cs_s.at[b, j], cs_r.at[b, j], sib)

    def c1(b):
        ref = A.at[b, 0, rows(q), :]
        send(ref, ref, cx_s.at[b, 0], cx_r.at[b, 0], xp)
        send(ref, ref, cy_s.at[b, 0, xh], cy_r.at[b, 0, xh], yp)
        send(ref, ref, cy_s.at[b, 1, xh], cy_r.at[b, 1, xh], ym)
        share(b, ref, q, 0)

    def c2(b):
        block = 2 * y + xo
        ref = A.at[b, 0, rows(block), :]
        got(ref, cx_s.at[b, 0], cx_r.at[b, 0])
        send(ref, ref, cy_s.at[b, 0, xo], cy_r.at[b, 0, xo], yp)
        send(ref, ref, cy_s.at[b, 1, xo], cy_r.at[b, 1, xo], ym)
        share(b, ref, block, 1)

    def c3(b):
        block = 2 * (y - 1)
        ref = A.at[b, 0, rows(block), :]
        got(ref, cy_s.at[b, 0, 0], cy_r.at[b, 0, 0])
        send(ref, ref, cr_s.at[b, 0], cr_r.at[b, 0], yp)
        share(b, ref, block, 2)
        block = 2 * (y + 1) + 1
        ref = A.at[b, 0, rows(block), :]
        got(ref, cy_s.at[b, 1, 1], cy_r.at[b, 1, 1])
        send(ref, ref, cr_s.at[b, 1], cr_r.at[b, 1], ym)
        share(b, ref, block, 3)

    def c4(b):
        for j, (block, sem_s, sem_r) in enumerate((
            (2 * (y - 1) + 1, cy_s.at[b, 0, 1], cy_r.at[b, 0, 1]),
            (2 * (y + 1), cy_s.at[b, 1, 0], cy_r.at[b, 1, 0]),
            (2 * (y + 2), cr_s.at[b, 0], cr_r.at[b, 0]),
            (2 * (y + 2) + 1, cr_s.at[b, 1], cr_r.at[b, 1]),
        )):
            ref = A.at[b, 0, rows(block), :]
            got(ref, sem_s, sem_r)
            share(b, ref, block, 4 + j)

    def c1x(b):
        ref = A.at[b, 0, rows(q), :]
        send(ref, ref, cy_s.at[b, 0, 0], cy_r.at[b, 0, 0], yp)
        send(ref, ref, cy_s.at[b, 1, 0], cy_r.at[b, 1, 0], ym)
        send(ref, ref, cx_s.at[b, 0], cx_r.at[b, 0], xp)
        share(b, ref, q, 0)

    def c2x(b):
        for side, sign, cols, to in ((0, -1, LOW, yp), (1, 1, HIGH, ym)):
            block = 2 * (y + sign) + xh
            ref = A.at[b, 0, rows(block), :]
            got(ref, cy_s.at[b, side, 0], cy_r.at[b, side, 0])
            part = A.at[b, 0, rows(block), cols]
            send(part, part, cr_s.at[b, side], cr_r.at[b, side], to)
            send(ref, ref, cx_s.at[b, 1 + side], cx_r.at[b, 1 + side], xp)
            share(b, ref, block, 1 + side)

    def c3x(b):
        block = 2 * (y + 2) + xh
        ref = A.at[b, 0, rows(block), :]
        got(A.at[b, 0, rows(block), LOW], cr_s.at[b, 0], cr_r.at[b, 0])
        got(A.at[b, 0, rows(block), HIGH], cr_s.at[b, 1], cr_r.at[b, 1])
        send(ref, ref, cx_s.at[b, 3], cx_r.at[b, 3], xp)
        share(b, ref, block, 3)

    def c4x(b):
        for j, place in enumerate((y, y - 1, y + 1, y + 2)):
            ref = A.at[b, 0, rows(2 * place + xo), :]
            got(ref, cx_s.at[b, j], cx_r.at[b, j])
            share(b, ref, 2 * place + xo, 4 + j)

    def c5(b):
        for j in range(8):
            got(A.at[b, 1, rows(q), :], cs_s.at[b, j], cs_r.at[b, j])

    def part_out():
        def tile(cols):
            acc = dot(A[0, 0], WdH[0, :, cols]) + dot(A[0, 1], WdH[1, :, cols])
            TT[0, :, cols] = acc.astype(BF)

        tiles(DW, 256, tile)

    def part_gate():
        def tile(cols):
            AC[:, cols] = dot_nt(A[1, 0], WgH[0, cols, :]) + dot_nt(A[1, 1], WgH[1, cols, :])

        tiles(DW, 256, tile)

    def part_grad():
        def tile(cols):
            acc = dot_nt(A[2, 0], WuH[0, cols, :]) + dot_nt(A[2, 1], WuH[1, cols, :])
            TT[1, :, cols] = (AC[:, cols] + acc).astype(BF)

        tiles(DW, 256, tile)

    def z_order(e):
        def tile(cols):
            OP[e, :, cols] = dot(PM[...], TT[e, :, cols]).astype(BF)

        tiles(DW, 256, tile)

    def d1(e):
        def out(block, side, j, to):
            send(OP.at[e, rows(block), :], RD.at[e, side, j], d_s.at[e, side, j], d_r.at[e, side, j], zat[to])

        far_side = e % 2
        sign = 1 if far_side == 0 else -1
        out(c + 4, far_side, 3, 2 * sign)
        out(c + 3, 0, 2, 1)
        out(c - 3, 1, 2, -1)
        out(c + 1, 0, 0, 1)
        out(c - 1, 1, 0, -1)

    def d_got(e, side, j):
        got(RD.at[e, side, j], d_s.at[e, side, j], d_r.at[e, side, j])
        return RD[e, side, j].astype(F32)

    def d2(e):
        for side, sign in ((0, 1), (1, -1)):
            acc = OP[e, rows(c + 2 * sign), :].astype(F32) + d_got(e, side, 2)
            if side == e % 2:
                acc += d_got(e, side, 3)
            ZS[e, side] = acc.astype(BF)
            send(ZS.at[e, side], RD.at[e, side, 1], d_s.at[e, side, 1], d_r.at[e, side, 1], zat[2 * sign])

    def residual(e):
        RES[e] = dot(PM[rows(c), :], G[0 if e == 0 else 2, 0])

    def d_last(e):
        full = OP[e, rows(c), :].astype(F32)
        full += d_got(e, 0, 0) + d_got(e, 1, 0) + d_got(e, 0, 1) + d_got(e, 1, 1)
        full = (full + RES[e]).astype(BF)
        for j in range(4):
            LS[e, j * B : (j + 1) * B, :] = full[:, j * 128 : (j + 1) * 128]

    def e_send(e):
        ES[e] = dot(SP[...], LS[e]).astype(BF)
        for j in range(16):
            there = pl.ds(pl.multiple_of(((r + j) % 16) * 16, 16), 16)
            here = pl.ds(pl.multiple_of(r * 16, 16), 16)
            send(ES.at[e, there, :], ED.at[e, here, :], e_s.at[e, j], e_r.at[e, j], far[j])

    def e_wait(e):
        for j in range(16):
            got(ED.at[e, pl.ds(0, 16), :], e_s.at[e, j], e_r.at[e, j])

    outs = []

    def put(src, dst):
        cp = pltpu.make_async_copy(src, dst, osem.at[len(outs)])
        cp.start()
        outs.append(cp)

    def grad_in(b, h):
        def tile(cols):
            GG[b - 1, h, :, cols] = dot(ST[...], A[b, h, :, cols]).astype(BF)

        tiles(H, 256, tile)
        put(GG.at[b - 1, h], (o_gg, o_gu)[b - 1].at[:, pl.ds((mine, other)[h], H)])

    def grad_out(h):
        def tile(cols):
            GD[h, cols, :] = lax.dot_general(
                A[3, h, :, cols], G[2, 0], (((0,), (0,)), ((), ())), preferred_element_type=F32
            ).astype(BF)

        tiles(H, 256, tile)
        put(GD.at[h], o_gd.at[pl.ds((mine, other)[h], H), :])

    z1(0)
    z1(1)
    send(wg.at[:, pl.ds(other, H)], WgX, wx_s.at[0], wx_r.at[0], sib)
    send(wu.at[:, pl.ds(other, H)], WuX, wx_s.at[1], wx_r.at[1], sib)
    z_near(0)
    z2(0)
    z1(2)
    load_down()
    z_near(1)
    z2(1)
    z3(0)
    loads[1].wait()
    got(WuX, wx_s.at[1], wx_r.at[1])
    z_shared(0)
    stage1(1)
    z_near(2)
    z2(2)
    loads[0].wait()
    got(WgX, wx_s.at[0], wx_r.at[0])
    stage1(0)
    z3(1)
    z_shared(1)
    stage1(3)
    z3(2)
    load_late()
    stage2(0)
    stage2x(1)
    stage1(2)
    loads[2].wait()
    got(WdX, wx_s.at[2], wx_r.at[2])
    z_shared(2)
    stage1(4)
    stage3(0)
    stage3x(1)
    stage2x(3)
    stage2(2)
    stage4(0)
    stage4x(1)
    activate_new()
    c1(0)
    stage2(4)
    stage3(2)
    stage3x(3)
    c2(0)
    stage3(4)
    c3(0)

    pi = lax.broadcasted_iota(jnp.int32, (T, T), 0)
    ti = lax.broadcasted_iota(jnp.int32, (T, T), 1)
    token = ((pi % B) // 3) * 24 + (pi // B) * 3 + pi % 3
    PM[...] = jnp.where(ti == token, 1.0, 0.0).astype(BF)
    ST[...] = jnp.transpose(G[1, 0])

    stage4(2)
    stage4x(3)
    stage4(4)
    activate_old()
    c1x(2)
    c1(1)
    c4(0)
    c2x(2)
    c2(1)
    for cp in loads[3:]:
        cp.wait()
    c3x(2)
    c3(1)
    c5(0)
    pl.semaphore_signal(row_sem, inc=1, device_id={"section": 1 - s}, device_id_type=MESH)
    part_out()
    z_order(0)
    d1(0)
    c4(1)
    c1x(3)
    residual(0)
    residual(1)
    c4x(2)
    c5(1)
    part_gate()
    c2x(3)
    d2(0)
    c5(2)
    part_grad()
    z_order(1)
    d1(1)
    d_last(0)

    ri = lax.broadcasted_iota(jnp.int32, (256, 4 * B), 0)
    li = lax.broadcasted_iota(jnp.int32, (256, 4 * B), 1)
    sub = ri % 16
    hit = (sub < 12) & (li // B == sub // 3) & (li % B == (ri // 16) * 3 + sub % 3)
    SP[...] = jnp.where(hit, 1.0, 0.0).astype(BF)

    pl.semaphore_wait(row_sem, 1)
    e_send(0)
    c3x(3)
    grad_in(1, 0)
    d2(1)
    c4x(3)
    grad_in(1, 1)
    grad_in(2, 0)
    d_last(1)
    e_send(1)
    grad_in(2, 1)
    c5(3)
    grad_out(0)
    grad_out(1)
    e_wait(0)
    e_wait(1)
    o_seen[...] = ED[...]
    for cp in outs:
        cp.wait()
    for cp in sent:
        cp.wait_send()


def finish(seen, gg, gu, gd, o_next, o_grad, o_gg, o_gu, o_gd, sem):
    copies = []
    for i, (src, dst) in enumerate(((gg, o_gg), (gu, o_gu), (gd, o_gd))):
        part = src.shape[0] // 4
        for j in range(4):
            here = pl.ds(j * part, part)
            cp = pltpu.make_async_copy(src.at[here, :], dst.at[0, here, :], sem.at[i, j])
            cp.start()
            copies.append(cp)
    for e, dst in enumerate((o_next, o_grad)):
        for j in range(16):
            for i in range(4):
                at = j * DW + i * 128
                dst[0, :, at : at + 128] = seen[e, j * 16 + i * 3 : j * 16 + i * 3 + 3, :]
    for cp in copies:
        cp.wait()


def body(fwd_in, bwd_in, cotangent, w_gate, w_up, w_down):
    vmem = pl.BlockSpec(memory_space=pltpu.VMEM)
    hbm = pl.BlockSpec(memory_space=pltpu.HBM)
    V = pltpu.VMEM
    D = pltpu.SemaphoreType.DMA
    scratch = [
        V((3, 2, T, DW), BF),
        V((2, DW, H), BF), V((2, DW, H), BF), V((2, H, DW), BF),
        V((DW, H), BF), V((DW, H), BF), V((H, DW), BF),
        V((5, T, H), BF),
        V((5, 2, B, H), BF), V((5, 2, B, H), BF), V((5, 2, B, H), BF), V((5, 2, B, H), BF),
        V((5, B, H), F32), V((5, B, H), BF), V((5, B, H), BF),
        V((2, 4, B, H), BF), V((2, 3, B, H), BF),
        V((4, 2, T, H), BF),
        V((2, T, DW), BF), V((T, DW), F32), V((2, T, DW), BF),
        V((2, 2, B, DW), BF), V((2, 2, 4, B, DW), BF),
        V((2, B, DW), F32), V((2, 4 * B, 128), BF), V((2, 256, 128), BF), V((2, 256, 128), BF),
        V((T, T), BF), V((256, 4 * B), BF), V((DW, T), BF),
        V((2, 2, DW, H), BF), V((2, H, DW), BF),
        D((6,)), D((3,)), D((3, 7)), D((3, 7)), D((3, 8)), D((3, 8)), D((3,)), D((3,)),
        D((5, 10)), D((5, 10)), D((4, 2, 2)), D((4, 2, 2)), D((4, 2)), D((4, 2)),
        D((4, 4)), D((4, 4)), D((4, 8)), D((4, 8)),
        D((2, 2, 4)), D((2, 2, 4)), D((2, 16)), D((2, 16)), D((6,)), pltpu.SemaphoreType.REGULAR,
    ]
    seen, gg, gu, gd = pl.pallas_call(
        kernel,
        out_shape=(
            jax.ShapeDtypeStruct((2, 256, 128), BF),
            jax.ShapeDtypeStruct((DW, 2 * H), BF),
            jax.ShapeDtypeStruct((DW, 2 * H), BF),
            jax.ShapeDtypeStruct((2 * H, DW), BF),
        ),
        in_specs=[vmem] * 3 + [hbm] * 3,
        out_specs=(vmem, hbm, hbm, hbm),
        scratch_shapes=scratch,
        compiler_params=pltpu.CompilerParams(
            collective_id=0, has_side_effects=True, vmem_limit_bytes=50 * 2**20
        ),
        cost_estimate=pl.CostEstimate(flops=8 * 10**9, bytes_accessed=12 * 10**6, transcendentals=0),
        name="relay",
    )(fwd_in[0], bwd_in[0], cotangent[0], w_gate[0], w_up[0], w_down[0])
    return pl.pallas_call(
        finish,
        out_shape=(
            jax.ShapeDtypeStruct((1, 3, 16 * DW), BF),
            jax.ShapeDtypeStruct((1, 3, 16 * DW), BF),
            jax.ShapeDtypeStruct((1, DW, 2 * H), BF),
            jax.ShapeDtypeStruct((1, DW, 2 * H), BF),
            jax.ShapeDtypeStruct((1, 2 * H, DW), BF),
        ),
        in_specs=[vmem, hbm, hbm, hbm],
        out_specs=(vmem, vmem, hbm, hbm, hbm),
        scratch_shapes=[pltpu.SemaphoreType.DMA((3, 4))],
        compiler_params=pltpu.CompilerParams(vmem_limit_bytes=16 * 2**20),
        name="finish",
    )(seen, gg, gu, gd)


def solution(mesh):
    in_specs = (
        P("section", "col", "row"),
        P("section", "col", "row"),
        P("section", "col", "row"),
        P("section", "row", "col"),
        P("section", "row", "col"),
        P("section", "col", "row"),
    )
    out_specs = (
        P("section", ("row", "col"), None),
        P("section", ("row", "col"), None),
        P("section", "row", "col"),
        P("section", "row", "col"),
        P("section", "col", "row"),
    )
    return jax.shard_map(body, mesh=mesh, in_specs=in_specs, out_specs=out_specs, check_vma=False)
```

time: 116 us -> 106 us (0.914)
  local copies, waits for them, and re-layouts: 9.36 us -> 3.88 us
  Pallas kernels: 106 us -> 101 us
    unnamed x9 -> x8, local copies, waits for them, and re-layouts: 9.36 us -> 3.88 us
    pallas_call x1 -> x2, Pallas kernels: 106 us -> 101 us  [the longest x1 98.2 us: body(): pl.pallas_call(kernel, out_shape=(jax.ShapeDtypeStruct((2, 256, 128), BF)...]
where the time goes in v2:
time: 106 us
  Pallas kernels  101 us (95%)
  local copies, waits for them, and re-layouts  3.88 us (4%)
    pallas_call x1, Pallas kernels, body(): pl.pallas_call(kernel, out_shape=(jax.ShapeDtypeStruct((2, 256, 128), BF)...  98.2 us
    unnamed x8, local copies, waits for them, and re-layouts  3.88 us
    pallas_call x1, Pallas kernels, body(): pl.pallas_call(finish, out_shape=(jax.ShapeDtypeStruct((1, 3, 16 * DW), B...  3.17 us

profile of v2, /device:TPU:1, one launch (start us, length us, event | category | flops | bytes accessed | tf_op | source)
XLA Modules:
  0.0 105.9 jit_solution(3967983500334691041)
XLA Ops:
  0.6 0.0 copy-start.1
  0.6 0.8 copy-done.1
  1.4 0.0 copy-start.2
  1.4 0.8 copy-done.2
  2.2 0.0 copy-start.3
  2.2 0.8 copy-done.3
  3.0 98.2 %relay.1 = (bf16[2,256,128]{2,1,0:T(8,128)(2,1)S(1)}, bf16[512,1792]{1,0:T(8,128)(2,1)S(1)}, bf16[512,1792]{1,0:T(8,128)(2,1)S(1)}, bf16[1792,512]{1,0:T(8,128)(2,1)}) custom-call(bf16[48,512]{1,0:T(8,128)(2,1)S(1)} %bitcast.6, bf16[48,512]{1,0:T(8,128)(2,1)S(1)} %bitcast.7, bf16[48,512]{1,0:T(8,128)(2,1)S(1)} %bitcast.8, bf16[512,1792]{1,0:T(8,128)(2,1)} %bitcast.9, ...), custom_call_target="tpu_custom_call" | custom-call | flops 8000000000 | bytes 12000000 | tf_op jit(solution)/shard_map/relay/pallas_call | solution.py:596
  101.3 0.0 copy-start
  101.3 1.5 %copy-done = bf16[1792,512]{1,0:T(8,128)(2,1)S(1)} copy-done((bf16[1792,512]{1,0:T(8,128)(2,1)S(1)}, bf16[1792,512]{1,0:T(8,128)(2,1)}, u32[]{:S(2)}) %copy-start) | copy-done | bytes 1835032
  102.8 3.2 %finish.1 = (bf16[1,3,8192]{2,1,0:T(4,128)(2,1)}, bf16[1,3,8192]{2,1,0:T(4,128)(2,1)}, bf16[1,512,1792]{2,1,0:T(8,128)(2,1)}, bf16[1,512,1792]{2,1,0:T(8,128)(2,1)}, bf16[1,1792,512]{2,1,0:T(8,128)(2,1)}) custom-call(bf16[2,256,128]{2,1,0:T(8,128)(2,1)S(1)} %get-tuple-element.9.seen, bf16[512,1792]{1,0:T(8,128)(2,1)S(1)} %get-tuple-element.10.gg, ...), custom_call_target="tpu_custom_call" | custom-call | tf_op jit(solution)/shard_map/finish/pallas_call | solution.py:613
Async XLA Ops:
  0.6 0.8 copy-start.1
  1.4 0.8 copy-start.2
  2.2 0.8 copy-start.3
  101.3 1.5 %copy-start = (bf16[1792,512]{1,0:T(8,128)(2,1)S(1)}, bf16[1792,512]{1,0:T(8,128)(2,1)}, u32[]{:S(2)}) copy-start(bf16[1792,512]{1,0:T(8,128)(2,1)} %get-tuple-element.12.gd) | copy-start | bytes 5505028

commit v3 on v2

--- a/solution.py
+++ b/solution.py
@@ -16,7 +16,6 @@
 H = 896
 LOW, HIGH = pl.ds(0, 512), pl.ds(512, 384)
 SUM_X = {1: 0, 3: 1}
-GATHER_X = (2, 3)
 
 
 def dot(left, right):
@@ -57,12 +56,13 @@
     sib = {"row": r + 1 - 2 * k}
     yp = {"row": ((y + 1) % 4) * 4 + xh * 2 + k}
     ym = {"row": ((y + 3) % 4) * 4 + xh * 2 + k}
+    y2 = {"row": ((y + 2) % 4) * 4 + xh * 2 + k}
     xp = {"row": y * 4 + xo * 2 + k}
     zat = {d: {"col": (c + d + 8) % 8} for d in (1, -1, 2, -2)}
     far = [{"section": 1 - s, "row": (r + j) % 16} for j in range(16)]
 
     barrier = pltpu.get_barrier_semaphore()
-    partners = [sib, yp, ym, xp, {"section": 1 - s}] + list(zat.values())
+    partners = [sib, yp, ym, y2, xp, {"section": 1 - s}] + list(zat.values())
     for d in partners:
         pl.semaphore_signal(barrier, inc=1, device_id=d, device_id_type=MESH)
 
@@ -106,7 +106,7 @@
             src_ref=ref, dst_ref=ref, send_sem=ssem, recv_sem=rsem, device_id=sib, device_id_type=MESH
         ).wait_recv()
 
-    xs = (x_new, x_old, x_cot)
+    xs = (x_old, x_cot, x_new)
     kept = []
     for a in range(3):
         cp = pltpu.make_async_copy(xs[a], G.at[a, 0, rows(c), :], xsem.at[a])
@@ -156,13 +156,13 @@
             got(G.at[a, 1, rows(c), :], gs_s.at[a, j], gs_r.at[a, j])
 
     def stage1(a):
-        if a == 4:
+        if a == 2:
             def tile(cols):
-                acc = dot_nt(G[2, 0], WdH[0, cols, :]) + dot_nt(G[2, 1], WdX[cols, :])
+                acc = dot_nt(G[1, 0], WdH[0, cols, :]) + dot_nt(G[1, 1], WdX[cols, :])
                 PS[a, :, cols] = acc.astype(BF)
         else:
-            own, theirs = ((WgH, WgX), (WuH, WuX))[a % 2]
-            t = a // 2
+            own, theirs = ((WgH, WgX), (WuH, WuX))[a % 3]
+            t = 0 if a < 2 else 2
 
             def tile(cols):
                 acc = dot(G[t, 0], own[0, :, cols]) + dot(G[t, 1], theirs[:, cols])
@@ -251,14 +251,14 @@
 
     def activate_new():
         def tile(cols):
-            gate, up = value(0, cols), value(1, cols)
+            gate, up = value(3, cols), value(4, cols)
             A[0, 0, rows(q), cols] = (gate * sigmoid(gate) * up).astype(BF)
 
         tiles(H, 128, tile)
 
     def activate_old():
         def tile(cols):
-            gate, up, d = value(2, cols), value(3, cols), value(4, cols)
+            gate, up, d = value(0, cols), value(1, cols), value(2, cols)
             sg = sigmoid(gate)
             A[1, 0, rows(q), cols] = (d * up * sg * (1.0 + gate * (1.0 - sg))).astype(BF)
             A[2, 0, rows(q), cols] = (d * gate * sg).astype(BF)
@@ -307,6 +307,16 @@
             got(ref, sem_s, sem_r)
             share(b, ref, block, 4 + j)
 
+    def direct(b, block, which):
+        ref = A.at[b, 0, rows(block), :]
+        send(ref, ref, cr_s.at[b, which], cr_r.at[b, which], y2)
+
+    def c3d(b):
+        for j, (block, side, which) in enumerate(((2 * (y - 1), 0, 0), (2 * (y + 1) + 1, 1, 1))):
+            ref = A.at[b, 0, rows(block), :]
+            got(ref, cy_s.at[b, side, which], cy_r.at[b, side, which])
+            share(b, ref, block, 2 + j)
+
     def c1x(b):
         ref = A.at[b, 0, rows(q), :]
         send(ref, ref, cy_s.at[b, 0, 0], cy_r.at[b, 0, 0], yp)
@@ -393,7 +403,7 @@
             send(ZS.at[e, side], RD.at[e, side, 1], d_s.at[e, side, 1], d_r.at[e, side, 1], zat[2 * sign])
 
     def residual(e):
-        RES[e] = dot(PM[rows(c), :], G[0 if e == 0 else 2, 0])
+        RES[e] = dot(PM[rows(c), :], G[2 if e == 0 else 1, 0])
 
     def d_last(e):
         full = OP[e, rows(c), :].astype(F32)
@@ -430,97 +440,24 @@
     def grad_out(h):
         def tile(cols):
             GD[h, cols, :] = lax.dot_general(
-                A[3, h, :, cols], G[2, 0], (((0,), (0,)), ((), ())), preferred_element_type=F32
+                A[3, h, :, cols], G[1, 0], (((0,), (0,)), ((), ())), preferred_element_type=F32
             ).astype(BF)
 
         tiles(H, 256, tile)
         put(GD.at[h], o_gd.at[pl.ds((mine, other)[h], H), :])
 
     z1(0)
-    z1(1)
+    send(wu.at[:, pl.ds(other, H)], WuX, wx_s.at[1], wx_r.at[1], sib)
     send(wg.at[:, pl.ds(other, H)], WgX, wx_s.at[0], wx_r.at[0], sib)
-    send(wu.at[:, pl.ds(other, H)], WuX, wx_s.at[1], wx_r.at[1], sib)
-    z_near(0)
-    z2(0)
-    z1(2)
-    load_down()
-    z_near(1)
-    z2(1)
-    z3(0)
-    loads[1].wait()
-    got(WuX, wx_s.at[1], wx_r.at[1])
-    z_shared(0)
-    stage1(1)
-    z_near(2)
-    z2(2)
-    loads[0].wait()
-    got(WgX, wx_s.at[0], wx_r.at[0])
-    stage1(0)
-    z3(1)
-    z_shared(1)
-    stage1(3)
-    z3(2)
-    load_late()
-    stage2(0)
-    stage2x(1)
-    stage1(2)
-    loads[2].wait()
-    got(WdX, wx_s.at[2], wx_r.at[2])
-    z_shared(2)
-    stage1(4)
-    stage3(0)
-    stage3x(1)
-    stage2x(3)
-    stage2(2)
-    stage4(0)
-    stage4x(1)
-    activate_new()
-    c1(0)
-    stage2(4)
-    stage3(2)
-    stage3x(3)
-    c2(0)
-    stage3(4)
-    c3(0)
 
     pi = lax.broadcasted_iota(jnp.int32, (T, T), 0)
     ti = lax.broadcasted_iota(jnp.int32, (T, T), 1)
     token = ((pi % B) // 3) * 24 + (pi // B) * 3 + pi % 3
     PM[...] = jnp.where(ti == token, 1.0, 0.0).astype(BF)
-    ST[...] = jnp.transpose(G[1, 0])
-
-    stage4(2)
-    stage4x(3)
-    stage4(4)
-    activate_old()
-    c1x(2)
-    c1(1)
-    c4(0)
-    c2x(2)
-    c2(1)
-    for cp in loads[3:]:
-        cp.wait()
-    c3x(2)
-    c3(1)
-    c5(0)
-    pl.semaphore_signal(row_sem, inc=1, device_id={"section": 1 - s}, device_id_type=MESH)
-    part_out()
-    z_order(0)
-    d1(0)
-    c4(1)
-    c1x(3)
-    residual(0)
-    residual(1)
-    c4x(2)
-    c5(1)
-    part_gate()
-    c2x(3)
-    d2(0)
-    c5(2)
-    part_grad()
-    z_order(1)
-    d1(1)
-    d_last(0)
+
+    z_near(0)
+    z2(0)
+    z1(1)
 
     ri = lax.broadcasted_iota(jnp.int32, (256, 4 * B), 0)
     li = lax.broadcasted_iota(jnp.int32, (256, 4 * B), 1)
@@ -528,16 +465,91 @@
     hit = (sub < 12) & (li // B == sub // 3) & (li % B == (ri // 16) * 3 + sub % 3)
     SP[...] = jnp.where(hit, 1.0, 0.0).astype(BF)
 
+    z3(0)
+    load_down()
+    z_near(1)
+    z2(1)
+    z1(2)
+    loads[1].wait()
+    got(WuX, wx_s.at[1], wx_r.at[1])
+    z_shared(0)
+    stage1(1)
+    loads[0].wait()
+    got(WgX, wx_s.at[0], wx_r.at[0])
+    stage1(0)
+    z_near(2)
+    z2(2)
+    z3(1)
+    loads[2].wait()
+    got(WdX, wx_s.at[2], wx_r.at[2])
+    z_shared(1)
+    stage1(2)
+    load_late()
+    stage2(0)
+    z3(2)
+    stage2x(1)
+    ST[...] = jnp.transpose(G[0, 0])
+    residual(1)
+    z_shared(2)
+    stage1(3)
+    stage1(4)
+    residual(0)
+    stage2(2)
+    stage3(0)
+    stage3x(1)
+    stage2x(3)
+    stage2(4)
+    stage3(2)
+    stage4(0)
+    stage4x(1)
+    stage4(2)
+    activate_old()
+    c1x(2)
+    c1(1)
+    stage3x(3)
+    stage3(4)
+    c2x(2)
+    c2(1)
+    c3x(2)
+    c3(1)
+    stage4x(3)
+    stage4(4)
+    activate_new()
+    c1(0)
+    direct(0, q, xh)
+    c4(1)
+    c2(0)
+    direct(0, 2 * y + xo, xo)
+    c4x(2)
+    for cp in loads[3:]:
+        cp.wait()
+    c5(1)
+    pl.semaphore_signal(row_sem, inc=1, device_id={"section": 1 - s}, device_id_type=MESH)
+    part_gate()
+    c5(2)
+    part_grad()
+    z_order(1)
+    d1(1)
+    c3d(0)
+    c4(0)
+    c1(3)
+    c5(0)
+    part_out()
+    z_order(0)
+    d1(0)
+    d2(1)
+    c2(3)
+    d2(0)
+    c3(3)
+    d_last(1)
     pl.semaphore_wait(row_sem, 1)
+    e_send(1)
+    grad_in(1, 0)
+    c4(3)
+    d_last(0)
     e_send(0)
-    c3x(3)
-    grad_in(1, 0)
-    d2(1)
-    c4x(3)
     grad_in(1, 1)
     grad_in(2, 0)
-    d_last(1)
-    e_send(1)
     grad_in(2, 1)
     c5(3)
     grad_out(0)
@@ -605,7 +617,7 @@
         out_specs=(vmem, hbm, hbm, hbm),
         scratch_shapes=scratch,
         compiler_params=pltpu.CompilerParams(
-            collective_id=0, has_side_effects=True, vmem_limit_bytes=50 * 2**20
+            collective_id=0, has_side_effects=True, vmem_limit_bytes=48 * 2**20
         ),
         cost_estimate=pl.CostEstimate(flops=8 * 10**9, bytes_accessed=12 * 10**6, transcendentals=0),
         name="relay",

time: 106 us -> 104 us (0.981)
  local copies, waits for them, and re-layouts: 3.88 us -> 2.39 us
    unnamed x8 -> x6, local copies, waits for them, and re-layouts: 3.88 us -> 2.39 us
where the time goes in v3:
time: 104 us
  Pallas kernels  101 us (97%)
  local copies, waits for them, and re-layouts  2.39 us (2%)
    pallas_call x1, Pallas kernels, body(): pl.pallas_call(kernel, out_shape=(jax.ShapeDtypeStruct((2, 256, 128), BF)...  97.8 us
    pallas_call x1, Pallas kernels, body(): pl.pallas_call(finish, out_shape=(jax.ShapeDtypeStruct((1, 3, 16 * DW), B...  3.17 us
    unnamed x6, local copies, waits for them, and re-layouts  2.39 us

profile of v3, /device:TPU:1, one launch (start us, length us, event | category | flops | bytes accessed | tf_op | source)
XLA Modules:
  0.0 104.0 jit_solution(7438400349353755536)
XLA Ops:
  0.6 0.0 copy-start
  0.6 0.8 copy-done
  1.4 0.0 copy-start.1
  1.4 0.8 copy-done.1
  2.2 0.0 copy-start.2
  2.2 0.8 copy-done.2
  3.0 97.8 %relay.1 = (bf16[2,256,128]{2,1,0:T(8,128)(2,1)S(1)}, bf16[512,1792]{1,0:T(8,128)(2,1)S(1)}, bf16[512,1792]{1,0:T(8,128)(2,1)S(1)}, bf16[1792,512]{1,0:T(8,128)(2,1)S(1)}) custom-call(bf16[48,512]{1,0:T(8,128)(2,1)S(1)} %bitcast.6, bf16[48,512]{1,0:T(8,128)(2,1)S(1)} %bitcast.7, bf16[48,512]{1,0:T(8,128)(2,1)S(1)} %bitcast.8, bf16[512,1792]{1,0:T(8,128)(2,1)} %bitcast.9, ...), custom_call_target="tpu_custom_call" | custom-call | flops 8000000000 | bytes 12000000 | tf_op jit(solution)/shard_map/relay/pallas_call | solution.py:608
  100.8 3.2 %finish.1 = (bf16[1,3,8192]{2,1,0:T(4,128)(2,1)}, bf16[1,3,8192]{2,1,0:T(4,128)(2,1)}, bf16[1,512,1792]{2,1,0:T(8,128)(2,1)}, bf16[1,512,1792]{2,1,0:T(8,128)(2,1)}, bf16[1,1792,512]{2,1,0:T(8,128)(2,1)}) custom-call(bf16[2,256,128]{2,1,0:T(8,128)(2,1)S(1)} %get-tuple-element.9.seen, bf16[512,1792]{1,0:T(8,128)(2,1)S(1)} %get-tuple-element.10.gg, ...), custom_call_target="tpu_custom_call" | custom-call | tf_op jit(solution)/shard_map/finish/pallas_call | solution.py:625
Async XLA Ops:
  0.6 0.8 copy-start
  1.4 0.8 copy-start.1
  2.2 0.8 copy-start.2

commit v4 on v3

--- a/solution.py
+++ b/solution.py
@@ -563,7 +563,7 @@
         cp.wait_send()
 
 
-def finish(seen, gg, gu, gd, o_next, o_grad, o_gg, o_gu, o_gd, sem):
+def finish(seen, gg, gu, gd, o_next, o_grad, o_gg, o_gu, o_gd, tok, sem, tsem):
     copies = []
     for i, (src, dst) in enumerate(((gg, o_gg), (gu, o_gu), (gd, o_gd))):
         part = src.shape[0] // 4
@@ -573,10 +573,14 @@
             cp.start()
             copies.append(cp)
     for e, dst in enumerate((o_next, o_grad)):
+        part = tok.at[e]
         for j in range(16):
             for i in range(4):
                 at = j * DW + i * 128
-                dst[0, :, at : at + 128] = seen[e, j * 16 + i * 3 : j * 16 + i * 3 + 3, :]
+                part[0, :, at : at + 128] = seen[e, j * 16 + i * 3 : j * 16 + i * 3 + 3, :]
+        cp = pltpu.make_async_copy(part, dst, tsem.at[e])
+        cp.start()
+        copies.append(cp)
     for cp in copies:
         cp.wait()
 
@@ -632,8 +636,8 @@
             jax.ShapeDtypeStruct((1, 2 * H, DW), BF),
         ),
         in_specs=[vmem, hbm, hbm, hbm],
-        out_specs=(vmem, vmem, hbm, hbm, hbm),
-        scratch_shapes=[pltpu.SemaphoreType.DMA((3, 4))],
+        out_specs=(hbm,) * 5,
+        scratch_shapes=[V((2, 1, 3, 16 * DW), BF), D((3, 4)), D((2,))],
         compiler_params=pltpu.CompilerParams(vmem_limit_bytes=16 * 2**20),
         name="finish",
     )(seen, gg, gu, gd)

time: 104 us -> 104 us (level)
  no operation moved by 1% of the time
where the time goes in v4:
time: 104 us; the launch traced here: 103 us
  Pallas kernels  100 us (96%)
  local copies, waits for them, and re-layouts  2.39 us (2%)
    pallas_call x1, Pallas kernels, body(): pl.pallas_call(kernel, out_shape=(jax.ShapeDtypeStruct((2, 256, 128), BF)...  97.8 us
    pallas_call x1, Pallas kernels, body(): pl.pallas_call(finish, out_shape=(jax.ShapeDtypeStruct((1, 3, 16 * DW), B...  2.56 us
    unnamed x6, local copies, waits for them, and re-layouts  2.39 us

profile of v4, /device:TPU:1, one launch (start us, length us, event | category | flops | bytes accessed | tf_op | source)
XLA Modules:
  0.0 103.4 jit_solution(4330046524476160789)
XLA Ops:
  0.6 0.0 copy-start
  0.6 0.8 copy-done
  1.4 0.0 copy-start.1
  1.4 0.8 copy-done.1
  2.2 0.0 copy-start.2
  2.2 0.8 copy-done.2
  3.0 97.8 %relay.1 = (bf16[2,256,128]{2,1,0:T(8,128)(2,1)S(1)}, bf16[512,1792]{1,0:T(8,128)(2,1)S(1)}, bf16[512,1792]{1,0:T(8,128)(2,1)S(1)}, bf16[1792,512]{1,0:T(8,128)(2,1)S(1)}) custom-call(bf16[48,512]{1,0:T(8,128)(2,1)S(1)} %bitcast.6, bf16[48,512]{1,0:T(8,128)(2,1)S(1)} %bitcast.7, bf16[48,512]{1,0:T(8,128)(2,1)S(1)} %bitcast.8, bf16[512,1792]{1,0:T(8,128)(2,1)} %bitcast.9, ...), custom_call_target="tpu_custom_call" | custom-call | flops 8000000000 | bytes 12000000 | tf_op jit(solution)/shard_map/relay/pallas_call | solution.py:612
  100.8 2.6 %finish.1 = (bf16[1,3,8192]{2,1,0:T(4,128)(2,1)}, bf16[1,3,8192]{2,1,0:T(4,128)(2,1)}, bf16[1,512,1792]{2,1,0:T(8,128)(2,1)}, bf16[1,512,1792]{2,1,0:T(8,128)(2,1)}, bf16[1,1792,512]{2,1,0:T(8,128)(2,1)}) custom-call(bf16[2,256,128]{2,1,0:T(8,128)(2,1)S(1)} %get-tuple-element.9.seen, bf16[512,1792]{1,0:T(8,128)(2,1)S(1)} %get-tuple-element.10.gg, ...), custom_call_target="tpu_custom_call" | custom-call | tf_op jit(solution)/shard_map/finish/pallas_call | solution.py:629
Async XLA Ops:
  0.6 0.8 copy-start
  1.4 0.8 copy-start.1
  2.2 0.8 copy-start.2
